TPU v7x, 32 devices: a whole 2x2x4 slice. The times are simulated.
32 devices in a mesh: shot: 8 (over y, x, core), space: 4 (over z).
Axes of the slice: x: 2, y: 2, z: 4, core: 2. Of those that a mesh axis runs over, the one named last changes fastest.
Arguments:
- courant: float32 [32, 128, 128], P('space'), may hold values from 0.03 to 0.18
- checkpoint: float32 [8, 2, 512, 8, 128], P('shot', None, 'space'), may hold values from -6 to 6
- block_target: int32 [8, 512], P('shot'), may hold values from 0 to 511, as said below
- adjoint_state: float32 [8, 2, 32, 128, 128], P('shot', None, 'space'), may hold values from -6 to 6
- wavelet: float32 [8, 4], P('shot'), may hold values from -8 to 8
- source_cell: int32 [8], P('shot'), may hold values from 0 to 524287
- receiver_cell: int32 [8, 512], P('shot'), may hold values from 0 to 524287
- residual: float32 [8, 4, 512], P('shot'), may hold values from -6 to 6
- check_rows: int32 [4, 64, 16], P('space'), may hold values from 0 to 1023
Outputs:
- gradient: float32 [32, 128, 128], P('space', 'shot')
- adjoint_carry: float32 [8, 2, 32, 128, 128], P('shot', None, 'space')
- checksums: float32 [4, 64, 128], P('space', 'shot')
Inputs may be any that keep to these rules, and one draw needn't show every extreme that they name: `block_target`: each shot's row is a permutation of the block positions. The stored blocks of one device (aligned blocks of 128 entries) name at most 32 positions of any one slab (128 consecutive positions); each device names exactly 32 of one slab, and each slab is named exactly 32 times by one device.
All inputs are finite; a program needn't handle non-finite values.
Results may differ from a plain program's by a relative error of at most 0.0003.
Values sent between devices are 32-bit elements; how exact they have to be, the bound alone decides.
A program may use at most 128 MiB of HBM per device.

v0:
```python
import jax
import jax.numpy as jnp
from jax import lax
from jax.sharding import PartitionSpec as P

STENCIL = (-205.0 / 72.0, 8.0 / 5.0, -1.0 / 5.0, 8.0 / 315.0, -1.0 / 560.0)


def padded_2(array, sides, width):
    for axis, dim in sides:
        devices, length = (lax.axis_size(axis), array.shape[dim])
        up = [(i, (i + 1) % devices) for i in range(devices - 1)]
        down = [(j, i) for i, j in up]
        last = lax.slice_in_dim(array, length - width, length, axis=dim)
        initial = lax.slice_in_dim(array, 0, width, axis=dim)
        before = lax.ppermute(last, axis, up)
        after = lax.ppermute(initial, axis, down)
        array = jnp.concatenate([before, array, after], axis=dim)
    return array


def laplace(field):
    length = field.shape[0] - 8
    height = field.shape[1]
    breadth = field.shape[2]
    padded = jnp.pad(field, ((0, 0), (4, 4), (4, 4)))
    summed = 3.0 * STENCIL[0] * padded[4 : 4 + length, 4 : 4 + height, 4 : 4 + breadth]
    for offset in range(1, 5):
        summed = summed + STENCIL[offset] * (
            padded[4 + offset : 4 + offset + length, 4 : 4 + height, 4 : 4 + breadth]
            + padded[4 - offset : 4 - offset + length, 4 : 4 + height, 4 : 4 + breadth]
        )
    for offset in range(1, 5):
        summed = summed + STENCIL[offset] * (
            padded[4 : 4 + length, 4 + offset : 4 + offset + height, 4 : 4 + breadth]
            + padded[4 : 4 + length, 4 - offset : 4 - offset + height, 4 : 4 + breadth]
        )
    for offset in range(1, 5):
        summed = summed + STENCIL[offset] * (
            padded[4 : 4 + length, 4 : 4 + height, 4 + offset : 4 + offset + breadth]
            + padded[4 : 4 + length, 4 : 4 + height, 4 - offset : 4 - offset + breadth]
        )
    return summed


def inject(field, cell_index, values, first_row):
    plane_cells = field.shape[1] * field.shape[2]
    local_cell = cell_index - first_row * plane_cells
    inside = (local_cell >= 0) & (local_cell < field.shape[0] * plane_cells)
    target = jnp.where(inside, local_cell, field.shape[0] * plane_cells)
    flattened = field.reshape(-1).at[target].add(values, mode="drop")
    return flattened.reshape(field.shape)


def advance(before, current_ext, courant, wave_value, source, first_row):
    following = 2.0 * current_ext[4:-4] - before + courant * laplace(current_ext)
    return inject(following, source, wave_value, first_row)


def retreat(following, current, weighted_ext, values, cell_index, first_row):
    earlier = 2.0 * current - following + laplace(weighted_ext)
    return inject(earlier, cell_index, values, first_row)


def extend(field):
    return padded_2(field, (("space", 0),), 4)


def body(
    courant,
    checkpoint,
    block_target,
    adjoint_state,
    wavelet,
    source_cell,
    receiver_cell,
    residual,
    check_rows,
):
    devices = lax.axis_size("space")
    position = lax.axis_index("space")
    length, height, breadth = courant.shape
    first_row = position * length
    per_device = checkpoint.shape[2]
    block_rows = checkpoint.shape[3]
    capacity = per_device // 4
    targets = block_target[0]
    payload = checkpoint[0]
    peers = targets // per_device
    matches = (peers[:, None] == jnp.arange(devices, dtype=jnp.int32)[None, :]).astype(jnp.int32)
    grouped = matches.reshape(devices, per_device, devices)
    ranking = jnp.sum((jnp.cumsum(grouped, axis=1) - grouped) * grouped, axis=2)
    peer_grid = peers.reshape(devices, per_device)
    own_peers = lax.dynamic_index_in_dim(peer_grid, position, 0, keepdims=False)
    own_ranks = lax.dynamic_index_in_dim(ranking, position, 0, keepdims=False)
    slot_of = own_peers * capacity + own_ranks
    outgoing = (
        jnp.zeros((2, devices * capacity, block_rows, breadth), jnp.float32)
        .at[:, slot_of]
        .set(payload)
    )
    outgoing = outgoing.reshape(2, devices, capacity, block_rows, breadth)
    incoming = lax.all_to_all(outgoing, "space", split_axis=1, concat_axis=1, tiled=True)
    incoming = incoming.reshape(2, devices * capacity, block_rows, breadth)
    sender_grid = jnp.arange(devices, dtype=jnp.int32)[:, None] * capacity + ranking
    owned = peer_grid == position
    local_block = (targets % per_device).reshape(devices, per_device)
    where_from = (
        jnp.zeros((per_device,), jnp.int32)
        .at[jnp.where(owned, local_block, per_device).reshape(-1)]
        .set(sender_grid.reshape(-1), mode="drop")
    )
    placed = jnp.take(incoming, where_from, axis=1)
    levels = placed.reshape(2, length, height, breadth)
    wavelet_row = wavelet[0]
    receivers = receiver_cell[0]
    traces = residual[0]
    horizon = wavelet_row.shape[0]
    fields = [levels[0], levels[1]]
    adjoints = [None] * (horizon + 2)
    adjoints[horizon + 1] = adjoint_state[0, 0]
    adjoints[horizon] = adjoint_state[0, 1]
    for moment in range(1, horizon + 1):
        fields.append(
            advance(
                fields[-2],
                extend(fields[-1]),
                courant,
                wavelet_row[moment - 1 : moment],
                source_cell,
                first_row,
            )
        )
    for moment in range(horizon, 0, -1):
        weighted = extend(courant * adjoints[moment])
        adjoints[moment - 1] = retreat(
            adjoints[moment + 1],
            adjoints[moment],
            weighted,
            traces[moment - 1],
            receivers,
            first_row,
        )
    partial_value = jnp.zeros((length, height, breadth), jnp.float32)
    for moment in range(1, horizon + 1):
        partial_value = partial_value + adjoints[moment] * (
            fields[moment + 1] - 2.0 * fields[moment] + fields[moment - 1]
        )
    slab_rows = partial_value.reshape(length * height, breadth)
    check_part = jnp.sum(slab_rows[check_rows[0]], axis=1)
    grad_share = lax.psum_scatter(partial_value, "shot", scatter_dimension=1, tiled=True)
    check_share = lax.psum_scatter(check_part, "shot", scatter_dimension=0, tiled=True)
    adjoint_carry = jnp.stack([adjoints[1], adjoints[0]])[None]
    return (grad_share, adjoint_carry, check_share[None])


def solution(mesh):
    in_specs = (
        P("space", None, None),
        P("shot", None, "space", None, None),
        P("shot", None),
        P("shot", None, "space", None, None),
        P("shot", None),
        P("shot"),
        P("shot", None),
        P("shot", None, None),
        P("space", None, None),
    )
    out_specs = (
        P("space", "shot", None),
        P("shot", None, "space", None, None),
        P("space", "shot", None),
    )
    return jax.shard_map(body, mesh=mesh, in_specs=in_specs, out_specs=out_specs, check_vma=False)
```

profile of v0, /device:TPU:0, one launch (start us, length us, event | category | flops | bytes accessed | tf_op | source)
XLA Modules:
  0.0 239.6 jit_solution(218769687859367359)
XLA Ops:
  7.2 1.3 bitcast_multiply_fusion.5
  8.5 4.9 %collective-permute-start.1 = (f32[4,128,128]{2,1,0:T(8,128)S(1)}, f32[4,128,128]{2,1,0:T(8,128)S(1)}, u32[]{:S(2)}, u32[]{:S(2)}) collective-permute-start(f32[4,128,128]{2,1,0:T(8,128)S(1)} %get-tuple-element.64), channel_id=1, source_target_pairs={{0,1},{1,2},{2,3},{4,5},{5,6},{6,7},{8,9},{9,10},{10,11},{12,13},{... | collective-permute-start | bytes 786440 | tf_op jit(solution)/shard_map/ppermute | solution.py:16
  13.4 1.3 collective-permute-start
  15.4 1.3 copy.14
  16.8 5.8 %scatter_fusion.3 = f32[2,128,8,128]{3,2,1,0:T(8,128)S(1)} fusion(f32[2,128,8,128]{3,2,1,0:T(8,128)S(1)} %broadcast_in_dim.48, s32[128]{0:T(128)S(1)} %fusion.306, f32[128,2,8,128]{3,2,1,0:T(8,128)S(1)} %copy.14), kind=kCustom, calls=%fused_computation.6 | custom fusion | bytes 3146240 | tf_op jit(solution)/shard_map/scatter | solution.py:100
  22.7 1.0 copy.15
  23.7 6.6 %all-to-all-start = ((f32[2,4,32,8,128]{4,3,2,0,1:T(8,128)}), f32[2,4,32,8,128]{4,3,2,0,1:T(8,128)}, u32[]{:S(2)}, u32[]{:S(2)}) async-start(f32[2,4,32,8,128]{4,3,2,0,1:T(8,128)} %copy.15), calls=%async_computation | async-start | bytes 2097152 | tf_op jit(solution)/shard_map/all_to_all | solution.py:103
  30.4 2.4 %scatter_custom_fusion.3 = s32[128]{0:T(128)S(1)} fusion(s32[512]{0:T(512)S(1)} %bitcast.210, s32[512]{0:T(512)S(1)} %add_bitcast_fusion, s32[]{:T(128)} %constant.151.clone.1), kind=kCustom, calls=%fused_computation.560 | custom fusion | bytes 516 | tf_op jit(solution)/shard_map/scatter | solution.py:111
  35.3 1.6 select_maximum_fusion.14
  36.9 3.4 %fusion.195 = f32[8,128,128]{2,1,0:T(8,128)S(1)} fusion(f32[8,128,128]{2,1,0:T(8,128)S(1)} %bitcast_multiply_fusion.5, f32[4,128,128]{2,1,0:T(8,128)S(1)} %collective-permute-done.1, f32[4,128,128]{2,1,0:T(8,128)} %collective-permute-done, f32[16,136,136]{2,1,0:T(8,128)S(1)} %select_maximum_fusion.14, f32[1,2,8,128,128]{4,3,2,1,0:T(8,128)} %param.20), kind=kLoop, calls=%fused_computation.321 | loop fusion | flops 6291456 | bytes 11010048 | tf_op jit(solution)/shard_map/add | solution.py:61
  40.4 3.5 %scatter_fusion = f32[131072]{0:T(1024)S(1)} fusion(f32[131072]{0:T(1024)S(1)} %bitcast.156, s32[512]{0:T(512)S(1)} %bitcast.201, f32[512]{0:T(512)S(1)} %bitcast.208), kind=kCustom, calls=%fused_computation.2 | custom fusion | flops 512 | bytes 8192 | tf_op jit(solution)/shard_map/scatter-add | solution.py:51
  44.1 4.1 %collective-permute-start.3 = (f32[4,128,128]{2,1,0:T(8,128)S(1)}, f32[4,128,128]{2,1,0:T(8,128)S(1)}, u32[]{:S(2)}, u32[]{:S(2)}) collective-permute-start(f32[4,128,128]{2,1,0:T(8,128)S(1)} %get-tuple-element.62), channel_id=1, source_target_pairs={{0,1},{1,2},{2,3},{4,5},{5,6},{6,7},{8,9},{9,10},{10,11},{12,13},{... | collective-permute-start | bytes 786440 | tf_op jit(solution)/shard_map/ppermute | solution.py:16
  48.2 1.3 collective-permute-start.2
  50.1 0.8 slice.924
  53.5 7.8 %collective-permute-done.2 = f32[4,128,128]{2,1,0:T(8,128)} collective-permute-done((f32[4,128,128]{2,1,0:T(8,128)S(1)}, f32[4,128,128]{2,1,0:T(8,128)}, u32[]{:S(2)}, u32[]{:S(2)}) %collective-permute-start.2) | collective-permute-done | bytes 262176 | tf_op jit(solution)/shard_map/ppermute | solution.py:17
  61.2 1.8 select_maximum_fusion.12
  63.0 2.3 copy.16
  65.3 3.0 %gather_fusion = f32[128,2,8,128]{3,2,1,0:T(8,128)} fusion(f32[2,128,8,128]{3,2,1,0:T(8,128)} %bitcast.195, s32[1024]{0:T(1024)} %pad_clamp_fusion), kind=kCustom, calls=%fused_computation | custom fusion | bytes 2097664 | tf_op jit(solution)/shard_map/jit(_take)/gather | solution.py:113
  68.3 1.4 select_bitcast_fusion
  69.8 2.5 %collective-permute-start.7 = (f32[4,128,128]{2,1,0:T(8,128)S(1)}, f32[4,128,128]{2,1,0:T(8,128)S(1)}, u32[]{:S(2)}, u32[]{:S(2)}) collective-permute-start(f32[4,128,128]{2,1,0:T(8,128)S(1)} %bitcast.200), channel_id=1, source_target_pairs={{0,1},{1,2},{2,3},{4,5},{5,6},{6,7},{8,9},{9,10},{10,11},{12,13},{... | collective-permute-start | bytes 786440 | tf_op jit(solution)/shard_map/ppermute | solution.py:16
  72.3 1.3 collective-permute-start.6
  73.6 0.9 fusion.309
  74.5 2.6 %collective-permute-done.7 = f32[4,128,128]{2,1,0:T(8,128)S(1)} collective-permute-done((f32[4,128,128]{2,1,0:T(8,128)S(1)}, f32[4,128,128]{2,1,0:T(8,128)S(1)}, u32[]{:S(2)}, u32[]{:S(2)}) %collective-permute-start.7) | collective-permute-done | bytes 262176 | tf_op jit(solution)/shard_map/ppermute | solution.py:16
  77.1 4.1 %collective-permute-done.6 = f32[4,128,128]{2,1,0:T(8,128)S(1)} collective-permute-done((f32[4,128,128]{2,1,0:T(8,128)S(1)}, f32[4,128,128]{2,1,0:T(8,128)S(1)}, u32[]{:S(2)}, u32[]{:S(2)}) %collective-permute-start.6) | collective-permute-done | bytes 262176 | tf_op jit(solution)/shard_map/ppermute | solution.py:17
  81.2 2.0 select_maximum_fusion.8
  83.3 11.9 %fusion.120 = f32[8,128,128]{2,1,0:T(8,128)S(1)} fusion(f32[8,128,128]{2,1,0:T(8,128)S(1)} %copy-done.3, f32[8,128,128]{2,1,0:T(8,128)S(1)} %bitcast.187, f32[4,128,128]{2,1,0:T(8,128)} %copy-done.22, f32[4,128,128]{2,1,0:T(8,128)} %copy-done.23, f32[16,136,136]{2,1,0:T(8,128)} %select_maximum_fusion.8, f32[8,128,128]{2,1,0:T(8,128)} %bitcast.193), kind=kLoop, calls=%fused_computation.246 | loop fusion | flops 6422528 | bytes 11010048 | tf_op jit(solution)/shard_map/add | solution.py:56
  95.2 2.0 fusion.302
  97.1 0.9 fusion.318
  98.0 2.8 %collective-permute-start.9 = (f32[4,128,128]{2,1,0:T(8,128)}, f32[4,128,128]{2,1,0:T(8,128)}, u32[]{:S(2)}, u32[]{:S(2)}) collective-permute-start(f32[4,128,128]{2,1,0:T(8,128)} %bitcast.34), channel_id=1, source_target_pairs={{0,1},{1,2},{2,3},{4,5},{5,6},{6,7},{8,9},{9,10},{10,11},{12,13},{... | collective-permute-start | bytes 786440 | tf_op jit(solution)/shard_map/ppermute | solution.py:16
  100.8 1.6 collective-permute-start.8
  102.4 3.4 %fusion.170 = f32[8,128,128]{2,1,0:T(8,128)S(1)} fusion(f32[8,128,128]{2,1,0:T(8,128)S(1)} %copy-done.17, f32[4,128,128]{2,1,0:T(8,128)S(1)} %collective-permute-done.3, f32[4,128,128]{2,1,0:T(8,128)} %collective-permute-done.2, f32[16,136,136]{2,1,0:T(8,128)S(1)} %select_maximum_fusion.12, f32[8,128,128]{2,1,0:T(8,128)S(1)} %bitcast.158, ...), kind=kLoop, calls=%fused_computation.296 | loop fusion | flops 6291456 | bytes 11010048 | tf_op jit(solution)/shard_map/add | solution.py:61
  105.9 3.5 %scatter_fusion.1 = f32[131072]{0:T(1024)S(1)} fusion(f32[131072]{0:T(1024)S(1)} %bitcast.161, s32[512]{0:T(512)S(1)} %bitcast.202, f32[512]{0:T(512)S(1)} %bitcast.207), kind=kCustom, calls=%fused_computation.3 | custom fusion | flops 512 | bytes 8192 | tf_op jit(solution)/shard_map/scatter-add | solution.py:51
  109.5 0.8 fusion.313
  110.4 4.6 %collective-permute-start.5 = (f32[4,128,128]{2,1,0:T(8,128)}, f32[4,128,128]{2,1,0:T(8,128)S(1)}, u32[]{:S(2)}, u32[]{:S(2)}) collective-permute-start(f32[4,128,128]{2,1,0:T(8,128)} %get-tuple-element.60), channel_id=1, source_target_pairs={{0,1},{1,2},{2,3},{4,5},{5,6},{6,7},{8,9},{9,10},{10,11},{12,13},{... | collective-permute-start | bytes 786440 | tf_op jit(solution)/shard_map/ppermute | solution.py:16
  114.9 1.3 collective-permute-start.4
  116.3 1.7 select_maximum_fusion.6
  117.9 3.5 %fusion.94 = f32[8,128,128]{2,1,0:T(8,128)S(1)} fusion(f32[8,128,128]{2,1,0:T(8,128)S(1)} %copy-done.5, f32[8,128,128]{2,1,0:T(8,128)S(1)} %bitcast.172, f32[4,128,128]{2,1,0:T(8,128)} %collective-permute-done.9, f32[4,128,128]{2,1,0:T(8,128)} %collective-permute-done.8, f32[16,136,136]{2,1,0:T(8,128)S(1)} %select_maximum_fusion.6, f32[8,128,128]{2,1,0:T(8,128)} %bitcast.188), kind=kLoop, calls=%fused_computation.220 | loop fusion | flops 6422528 | bytes 11010048 | tf_op jit(solution)/shard_map/add | solution.py:56
  121.5 2.0 fusion.303
  123.5 4.6 %collective-permute-start.11 = (f32[4,128,128]{2,1,0:T(8,128)S(1)}, f32[4,128,128]{2,1,0:T(8,128)S(1)}, u32[]{:S(2)}, u32[]{:S(2)}) collective-permute-start(f32[4,128,128]{2,1,0:T(8,128)S(1)} %bitcast.198), channel_id=1, source_target_pairs={{0,1},{1,2},{2,3},{4,5},{5,6},{6,7},{8,9},{9,10},{10,11},{12,13},{... | collective-permute-start | bytes 786440 | tf_op jit(solution)/shard_map/ppermute | solution.py:16
  128.1 1.3 collective-permute-start.10
  129.4 1.8 select_maximum_fusion.10
  131.9 4.4 %collective-permute-done.10 = f32[4,128,128]{2,1,0:T(8,128)S(1)} collective-permute-done((f32[4,128,128]{2,1,0:T(8,128)S(1)}, f32[4,128,128]{2,1,0:T(8,128)S(1)}, u32[]{:S(2)}, u32[]{:S(2)}) %collective-permute-start.10) | collective-permute-done | bytes 262176 | tf_op jit(solution)/shard_map/ppermute | solution.py:17
  137.0 2.0 select_maximum_fusion.4
  139.1 12.5 %fusion.68 = f32[8,128,128]{2,1,0:T(8,128)} fusion(f32[8,128,128]{2,1,0:T(8,128)S(1)} %copy-done.5, f32[8,128,128]{2,1,0:T(8,128)S(1)} %bitcast.177, f32[4,128,128]{2,1,0:T(8,128)} %copy-done.20, f32[4,128,128]{2,1,0:T(8,128)} %copy-done.21, f32[16,136,136]{2,1,0:T(8,128)} %select_maximum_fusion.4, f32[8,128,128]{2,1,0:T(8,128)S(1)} %bitcast.173), kind=kLoop, calls=%fused_computation.194 | loop fusion | flops 6422528 | bytes 11010048 | tf_op jit(solution)/shard_map/add | solution.py:56
  151.6 3.2 %fusion.304 = f32[131072]{0:T(1024)} fusion(f32[131072]{0:T(1024)} %bitcast.180, s32[]{:T(128)} %bitcast.30, f32[1,1]{1,0:T(1,128)} %get-tuple-element.78, s32[1]{0:T(128)} %compare_select_fusion.7), kind=kLoop, calls=%fused_computation.556 | loop fusion | flops 5 | bytes 2560 | tf_op jit(solution)/shard_map/scatter-add | solution.py:51
  154.8 1.9 fusion.316
  156.7 2.6 %collective-permute-start.13 = (f32[4,128,128]{2,1,0:T(8,128)}, f32[4,128,128]{2,1,0:T(8,128)}, u32[]{:S(2)}, u32[]{:S(2)}) collective-permute-start(f32[4,128,128]{2,1,0:T(8,128)} %bitcast.44), channel_id=1, source_target_pairs={{0,1},{1,2},{2,3},{4,5},{5,6},{6,7},{8,9},{9,10},{10,11},{12,13},{... | collective-permute-start | bytes 786440 | tf_op jit(solution)/shard_map/ppermute | solution.py:16
  159.3 1.4 collective-permute-start.12
  160.7 5.0 %fusion.145 = f32[8,128,128]{2,1,0:T(8,128)} fusion(f32[8,128,128]{2,1,0:T(8,128)} %copy-done.18, f32[4,128,128]{2,1,0:T(8,128)S(1)} %collective-permute-done.5, f32[4,128,128]{2,1,0:T(8,128)} %collective-permute-done.4, f32[16,136,136]{2,1,0:T(8,128)S(1)} %select_maximum_fusion.10, f32[8,128,128]{2,1,0:T(8,128)S(1)} %bitcast.159, ...), kind=kLoop, calls=%fused_computation.271 | loop fusion | flops 6291456 | bytes 11010048 | tf_op jit(solution)/shard_map/add | solution.py:61
  165.7 4.8 %scatter_fusion.2 = f32[131072]{0:T(1024)} fusion(f32[131072]{0:T(1024)} %bitcast.166, s32[512]{0:T(512)S(1)} %bitcast.203, f32[512]{0:T(512)S(1)} %bitcast.206), kind=kCustom, calls=%fused_computation.4 | custom fusion | flops 512 | bytes 8192 | tf_op jit(solution)/shard_map/scatter-add | solution.py:51
  170.5 1.9 select_maximum_fusion.2
  172.4 5.1 %fusion.42 = f32[8,128,128]{2,1,0:T(8,128)} fusion(f32[8,128,128]{2,1,0:T(8,128)S(1)} %copy-done.6, f32[8,128,128]{2,1,0:T(8,128)} %bitcast.182, f32[4,128,128]{2,1,0:T(8,128)} %collective-permute-done.13, f32[4,128,128]{2,1,0:T(8,128)} %collective-permute-done.12, f32[16,136,136]{2,1,0:T(8,128)S(1)} %select_maximum_fusion.2, f32[8,128,128]{2,1,0:T(8,128)} %bitcast.178), kind=kLoop, calls=%fused_computation.168 | loop fusion | flops 6422528 | bytes 11010048 | tf_op jit(solution)/shard_map/add | solution.py:56
  177.5 3.3 %fusion.305 = f32[131072]{0:T(1024)} fusion(f32[131072]{0:T(1024)} %bitcast.191, s32[]{:T(128)} %bitcast.30, f32[1,1]{1,0:T(1,128)} %get-tuple-element.75, s32[1]{0:T(128)} %compare_select_fusion.7), kind=kLoop, calls=%fused_computation.557 | loop fusion | flops 5 | bytes 2560 | tf_op jit(solution)/shard_map/scatter-add | solution.py:51
  180.9 3.3 %fusion.312 = (f32[8,128,128]{2,1,0:T(8,128)S(1)}, f32[8,128,128]{2,1,0:T(8,128)}) fusion(f32[8,128,128]{2,1,0:T(8,128)S(1)} %copy-done.6, f32[8,128,128]{2,1,0:T(8,128)S(1)} %bitcast.167, f32[8,128,128]{2,1,0:T(8,128)} %bitcast.179, f32[8,128,128]{2,1,0:T(8,128)} %bitcast.192, f32[8,128,128]{2,1,0:T(8,128)} %bitcast.183, f32[1,2,8,128,128]{4,3,2,1,0:T(8,128)} %param.20, ...), kind=kLoop, calls=%fused_computation.565 | loop fusion | flops 2621440 | bytes 6815744 | tf_op jit(solution)/shard_map/mul | solution.py:135
  184.3 0.9 fusion.311
  185.2 4.6 %collective-permute-start.15 = (f32[4,128,128]{2,1,0:T(8,128)}, f32[4,128,128]{2,1,0:T(8,128)S(1)}, u32[]{:S(2)}, u32[]{:S(2)}) collective-permute-start(f32[4,128,128]{2,1,0:T(8,128)} %get-tuple-element.56), channel_id=1, source_target_pairs={{0,1},{1,2},{2,3},{4,5},{5,6},{6,7},{8,9},{9,10},{10,11},{12,13},{... | collective-permute-start | bytes 786440 | tf_op jit(solution)/shard_map/ppermute | solution.py:16
  189.7 1.3 collective-permute-start.14
  191.0 2.1 fusion.289
  193.1 2.8 %gather_fusion.1 = f32[1024,128]{1,0:T(8,128)S(1)} fusion(f32[1024,128]{1,0:T(8,128)S(1)} %fusion.289, s32[1024]{0:T(1024)S(1)} %broadcast_clamp_fusion), kind=kCustom, calls=%fused_computation.1 | custom fusion | bytes 1052672 | tf_op jit(solution)/shard_map/gather | solution.py:150
  196.0 22.6 %all-reduce.8 = f32[64,128]{1,0:T(8,128)S(1)} all-reduce(f32[64,128]{1,0:T(8,128)S(1)} %bitcast_reduce_fusion), channel_id=3, replica_groups=mesh['shot'=8,'space'=4] {'shot'}, use_global_device_ids=true, to_apply=%region_10.11.clone | all-reduce | flops 8192 | bytes 65536
  219.2 1.8 select_maximum_fusion
  221.0 4.8 %fusion.16 = f32[8,128,128]{2,1,0:T(8,128)} fusion(f32[8,128,128]{2,1,0:T(8,128)} %copy-done.19, f32[4,128,128]{2,1,0:T(8,128)S(1)} %collective-permute-done.15, f32[4,128,128]{2,1,0:T(8,128)} %collective-permute-done.14, f32[16,136,136]{2,1,0:T(8,128)S(1)} %select_maximum_fusion, f32[8,128,128]{2,1,0:T(8,128)S(1)} %bitcast.165, f32[8,128,128]{2,1,0:T(8,128)S(1)} %bitcast.168), kind=kLoop, calls=%fused_computation.142 | loop fusion | flops 6291456 | bytes 11010048 | tf_op jit(solution)/shard_map/add | solution.py:61
  225.8 4.8 %scatter_fusion.4 = f32[131072]{0:T(1024)} fusion(f32[131072]{0:T(1024)} %bitcast.184, s32[512]{0:T(512)S(1)} %bitcast.204, f32[512]{0:T(512)S(1)} %bitcast.205), kind=kCustom, calls=%fused_computation.7 | custom fusion | flops 512 | bytes 8192 | tf_op jit(solution)/shard_map/scatter-add | solution.py:51
  230.7 2.1 maximum_bitcast_fusion
  (114 shorter events, 7.2 us)
Async XLA Ops:
  7.2 7.6 %copy-start.29 = (s32[1,512]{1,0:T(1,128)S(1)}, s32[1,512]{1,0:T(1,128)}, u32[]{:S(2)}) copy-start(s32[1,512]{1,0:T(1,128)} %param.19) | copy-start | bytes 6148
  8.5 26.8 %collective-permute-start.1 = (f32[4,128,128]{2,1,0:T(8,128)S(1)}, f32[4,128,128]{2,1,0:T(8,128)S(1)}, u32[]{:S(2)}, u32[]{:S(2)}) collective-permute-start(f32[4,128,128]{2,1,0:T(8,128)S(1)} %get-tuple-element.64), channel_id=1, source_target_pairs={{0,1},{1,2},{2,3},{4,5},{5,6},{6,7},{8,9},{9,10},{10,11},{12,13},{... | collective-permute-start | bytes 786440 | tf_op jit(solution)/shard_map/ppermute | solution.py:16
  13.4 21.9 %collective-permute-start = (f32[4,128,128]{2,1,0:T(8,128)S(1)}, f32[4,128,128]{2,1,0:T(8,128)}, u32[]{:S(2)}, u32[]{:S(2)}) collective-permute-start(f32[4,128,128]{2,1,0:T(8,128)S(1)} %get-tuple-element.63), channel_id=1, source_target_pairs={{1,0},{2,1},{3,2},{5,4},{6,5},{7,6},{9,8},{10,9},{11,10},{13,12},{... | collective-permute-start | bytes 786440 | tf_op jit(solution)/shard_map/ppermute | solution.py:17
  22.6 11.4 %copy-start.27 = (f32[1,4,512]{2,1,0:T(4,128)S(1)}, f32[1,4,512]{2,1,0:T(4,128)}, u32[]{:S(2)}) copy-start(f32[1,4,512]{2,1,0:T(4,128)} %param.24) | copy-start | bytes 24580
  22.7 11.9 %copy-start.31 = (s32[1,512]{1,0:T(1,128)S(1)}, s32[1,512]{1,0:T(1,128)}, u32[]{:S(2)}) copy-start(s32[1,512]{1,0:T(1,128)} %param.23) | copy-start | bytes 6148
  22.7 11.9 %copy-start.30 = (f32[1,4]{1,0:T(1,128)S(1)}, f32[1,4]{1,0:T(1,128)}, u32[]{:S(2)}) copy-start(f32[1,4]{1,0:T(1,128)} %param.21) | copy-start | bytes 52
  22.7 12.6 %copy-start.28 = (s32[1,64,16]{1,2,0:T(8,128)S(1)}, s32[1,64,16]{1,2,0:T(8,128)}, u32[]{:S(2)}) copy-start(s32[1,64,16]{1,2,0:T(8,128)} %param.25) | copy-start | bytes 12292
  23.7 39.3 %all-to-all-start = ((f32[2,4,32,8,128]{4,3,2,0,1:T(8,128)}), f32[2,4,32,8,128]{4,3,2,0,1:T(8,128)}, u32[]{:S(2)}, u32[]{:S(2)}) async-start(f32[2,4,32,8,128]{4,3,2,0,1:T(8,128)} %copy.15), calls=%async_computation | async-start | bytes 2097152 | tf_op jit(solution)/shard_map/all_to_all | solution.py:103
  30.3 202.4 %reduce-scatter.2.cloned.1.call-start = ((), (), s32[]{:S(2)}) async-start(), calls=%async_computation.2 | async-start | bytes 589824 | tf_op jit(solution)/shard_map/reduce_scatter | solution.py:151
  40.4 3.6 %copy-start.3 = (f32[8,128,128]{2,1,0:T(8,128)S(1)}, f32[8,128,128]{2,1,0:T(8,128)}, u32[]{:S(2)}) copy-start(f32[8,128,128]{2,1,0:T(8,128)} %param.17) | copy-start | bytes 1572868
  43.9 5.6 %copy-start.33 = (s32[128]{0:T(128)S(1)}, s32[128]{0:T(128)}, u32[]{:S(2)}) copy-start(s32[128]{0:T(128)} %compare_select_fusion.9) | copy-start | bytes 1540
  44.0 6.1 %copy-start.15 = (f32[1,2,8,128,128]{4,3,2,1,0:T(8,128)S(1)}, f32[1,2,8,128,128]{4,3,2,1,0:T(8,128)}, u32[]{:S(2)}) copy-start(f32[1,2,8,128,128]{4,3,2,1,0:T(8,128)} %param.20) | copy-start | bytes 3145732
  44.0 8.3 %copy-start.34 = (u32[32]{0:T(128)S(1)}, u32[32]{0:T(128)}, u32[]{:S(2)}) copy-start(u32[32]{0:T(128)} %constant.190) | copy-start | bytes 388
  44.1 6.9 %copy-start.16 = (f32[8,128,128]{2,1,0:T(8,128)}, f32[8,128,128]{2,1,0:T(8,128)S(1)}, u32[]{:S(2)}) copy-start(f32[8,128,128]{2,1,0:T(8,128)S(1)} %mul.453) | copy-start | bytes 1572868
  44.1 9.3 %collective-permute-start.3 = (f32[4,128,128]{2,1,0:T(8,128)S(1)}, f32[4,128,128]{2,1,0:T(8,128)S(1)}, u32[]{:S(2)}, u32[]{:S(2)}) collective-permute-start(f32[4,128,128]{2,1,0:T(8,128)S(1)} %get-tuple-element.62), channel_id=1, source_target_pairs={{0,1},{1,2},{2,3},{4,5},{5,6},{6,7},{8,9},{9,10},{10,11},{12,13},{... | collective-permute-start | bytes 786440 | tf_op jit(solution)/shard_map/ppermute | solution.py:16
  48.2 13.0 %collective-permute-start.2 = (f32[4,128,128]{2,1,0:T(8,128)S(1)}, f32[4,128,128]{2,1,0:T(8,128)}, u32[]{:S(2)}, u32[]{:S(2)}) collective-permute-start(f32[4,128,128]{2,1,0:T(8,128)S(1)} %get-tuple-element.61), channel_id=1, source_target_pairs={{1,0},{2,1},{3,2},{5,4},{6,5},{7,6},{9,8},{10,9},{11,10},{13,12},{... | collective-permute-start | bytes 786440 | tf_op jit(solution)/shard_map/ppermute | solution.py:17
  63.0 5.3 %copy-start.32 = (pred[128]{0:T(512)(128)(4,1)S(1)}, pred[128]{0:T(512)(128)(4,1)}, u32[]{:S(2)}) copy-start(pred[128]{0:T(512)(128)(4,1)} %compare_and_fusion.1) | copy-start | bytes 388
  69.7 3.9 %copy-start.14 = (f32[2,128,8,128]{3,2,0,1:T(8,128)}, f32[2,128,8,128]{3,2,0,1:T(8,128)S(1)}, u32[]{:S(2)}) copy-start(f32[2,128,8,128]{3,2,0,1:T(8,128)S(1)} %select_bitcast_fusion) | copy-start | bytes 3145732
  69.8 7.3 %collective-permute-start.7 = (f32[4,128,128]{2,1,0:T(8,128)S(1)}, f32[4,128,128]{2,1,0:T(8,128)S(1)}, u32[]{:S(2)}, u32[]{:S(2)}) collective-permute-start(f32[4,128,128]{2,1,0:T(8,128)S(1)} %bitcast.200), channel_id=1, source_target_pairs={{0,1},{1,2},{2,3},{4,5},{5,6},{6,7},{8,9},{9,10},{10,11},{12,13},{... | collective-permute-start | bytes 786440 | tf_op jit(solution)/shard_map/ppermute | solution.py:16
  72.3 8.9 %collective-permute-start.6 = (f32[4,128,128]{2,1,0:T(8,128)S(1)}, f32[4,128,128]{2,1,0:T(8,128)S(1)}, u32[]{:S(2)}, u32[]{:S(2)}) collective-permute-start(f32[4,128,128]{2,1,0:T(8,128)S(1)} %bitcast.199), channel_id=1, source_target_pairs={{1,0},{2,1},{3,2},{5,4},{6,5},{7,6},{9,8},{10,9},{11,10},{13,12},{... | collective-permute-start | bytes 786440 | tf_op jit(solution)/shard_map/ppermute | solution.py:17
  74.5 20.6 %copy-start.13 = (f32[1,128,8,128]{3,2,0,1:T(8,128)}, f32[1,128,8,128]{3,2,0,1:T(8,128)S(1)}, u32[]{:S(2)}) copy-start(f32[1,128,8,128]{3,2,0,1:T(8,128)S(1)} %get-tuple-element.52) | copy-start | bytes 1572868
  77.1 6.2 %copy-start.22 = (f32[4,128,128]{2,1,0:T(8,128)}, f32[4,128,128]{2,1,0:T(8,128)S(1)}, u32[]{:S(2)}) copy-start(f32[4,128,128]{2,1,0:T(8,128)S(1)} %collective-permute-done.7) | copy-start | bytes 786436
  81.2 2.0 copy-start.23
  83.3 19.2 %copy-start.17 = (f32[8,128,128]{2,1,0:T(8,128)S(1)}, f32[8,128,128]{2,1,0:T(8,128)}, u32[]{:S(2)}) copy-start(f32[8,128,128]{2,1,0:T(8,128)} %copy-done.16) | copy-start | bytes 1572868
  97.1 8.7 %copy-start.7 = (f32[131072]{0:T(1024)}, f32[131072]{0:T(1024)S(1)}, u32[]{:S(2)}) copy-start(f32[131072]{0:T(1024)S(1)} %fusion.302) | copy-start | bytes 1572868
  98.0 18.2 %collective-permute-start.9 = (f32[4,128,128]{2,1,0:T(8,128)}, f32[4,128,128]{2,1,0:T(8,128)}, u32[]{:S(2)}, u32[]{:S(2)}) collective-permute-start(f32[4,128,128]{2,1,0:T(8,128)} %bitcast.34), channel_id=1, source_target_pairs={{0,1},{1,2},{2,3},{4,5},{5,6},{6,7},{8,9},{9,10},{10,11},{12,13},{... | collective-permute-start | bytes 786440 | tf_op jit(solution)/shard_map/ppermute | solution.py:16
  100.8 5.0 %copy-start.26 = (f32[1,1,512]{2,1,0:T(1,128)S(1)}, f32[1,1,512]{2,1,0:T(1,128)}, u32[]{:S(2)}) copy-start(f32[1,1,512]{2,1,0:T(1,128)} %get-tuple-element.72) | copy-start | bytes 6148
  100.8 15.4 %collective-permute-start.8 = (f32[4,128,128]{2,1,0:T(8,128)}, f32[4,128,128]{2,1,0:T(8,128)}, u32[]{:S(2)}, u32[]{:S(2)}) collective-permute-start(f32[4,128,128]{2,1,0:T(8,128)} %bitcast.33), channel_id=1, source_target_pairs={{1,0},{2,1},{3,2},{5,4},{6,5},{7,6},{9,8},{10,9},{11,10},{13,12},{... | collective-permute-start | bytes 786440 | tf_op jit(solution)/shard_map/ppermute | solution.py:17
  105.8 3.6 %copy-start.4 = (f32[8,128,128]{2,1,0:T(8,128)S(1)}, f32[8,128,128]{2,1,0:T(8,128)}, u32[]{:S(2)}) copy-start(f32[8,128,128]{2,1,0:T(8,128)} %param.17) | copy-start | bytes 1572868
  109.4 6.8 %copy-start.8 = (f32[131072]{0:T(1024)S(1)}, f32[131072]{0:T(1024)}, u32[]{:S(2)}) copy-start(f32[131072]{0:T(1024)} %copy-done.7) | copy-start | bytes 1572868
  109.5 6.7 %copy-start.18 = (f32[8,128,128]{2,1,0:T(8,128)}, f32[8,128,128]{2,1,0:T(8,128)S(1)}, u32[]{:S(2)}) copy-start(f32[8,128,128]{2,1,0:T(8,128)S(1)} %mul.468) | copy-start | bytes 1572868
  109.5 8.4 %copy-start.5 = (f32[8,128,128]{2,1,0:T(8,128)S(1)}, f32[8,128,128]{2,1,0:T(8,128)}, u32[]{:S(2)}) copy-start(f32[8,128,128]{2,1,0:T(8,128)} %param.17) | copy-start | bytes 1572868
  110.4 19.0 %collective-permute-start.5 = (f32[4,128,128]{2,1,0:T(8,128)}, f32[4,128,128]{2,1,0:T(8,128)S(1)}, u32[]{:S(2)}, u32[]{:S(2)}) collective-permute-start(f32[4,128,128]{2,1,0:T(8,128)} %get-tuple-element.60), channel_id=1, source_target_pairs={{0,1},{1,2},{2,3},{4,5},{5,6},{6,7},{8,9},{9,10},{10,11},{12,13},{... | collective-permute-start | bytes 786440 | tf_op jit(solution)/shard_map/ppermute | solution.py:16
  114.9 14.5 %collective-permute-start.4 = (f32[4,128,128]{2,1,0:T(8,128)}, f32[4,128,128]{2,1,0:T(8,128)}, u32[]{:S(2)}, u32[]{:S(2)}) collective-permute-start(f32[4,128,128]{2,1,0:T(8,128)} %get-tuple-element.59), channel_id=1, source_target_pairs={{1,0},{2,1},{3,2},{5,4},{6,5},{7,6},{9,8},{10,9},{11,10},{13,12},{... | collective-permute-start | bytes 786440 | tf_op jit(solution)/shard_map/ppermute | solution.py:17
  123.5 15.6 %copy-start.11 = (f32[131072]{0:T(1024)}, f32[131072]{0:T(1024)S(1)}, u32[]{:S(2)}) copy-start(f32[131072]{0:T(1024)S(1)} %fusion.303) | copy-start | bytes 1572868
  123.5 8.4 %collective-permute-start.11 = (f32[4,128,128]{2,1,0:T(8,128)S(1)}, f32[4,128,128]{2,1,0:T(8,128)S(1)}, u32[]{:S(2)}, u32[]{:S(2)}) collective-permute-start(f32[4,128,128]{2,1,0:T(8,128)S(1)} %bitcast.198), channel_id=1, source_target_pairs={{0,1},{1,2},{2,3},{4,5},{5,6},{6,7},{8,9},{9,10},{10,11},{12,13},{... | collective-permute-start | bytes 786440 | tf_op jit(solution)/shard_map/ppermute | solution.py:16
  128.1 8.3 %collective-permute-start.10 = (f32[4,128,128]{2,1,0:T(8,128)S(1)}, f32[4,128,128]{2,1,0:T(8,128)S(1)}, u32[]{:S(2)}, u32[]{:S(2)}) collective-permute-start(f32[4,128,128]{2,1,0:T(8,128)S(1)} %bitcast.197), channel_id=1, source_target_pairs={{1,0},{2,1},{3,2},{5,4},{6,5},{7,6},{9,8},{10,9},{11,10},{13,12},{... | collective-permute-start | bytes 786440 | tf_op jit(solution)/shard_map/ppermute | solution.py:17
  131.9 4.4 %copy-start.20 = (f32[4,128,128]{2,1,0:T(8,128)}, f32[4,128,128]{2,1,0:T(8,128)S(1)}, u32[]{:S(2)}) copy-start(f32[4,128,128]{2,1,0:T(8,128)S(1)} %collective-permute-done.11) | copy-start | bytes 786436
  136.3 0.7 copy-start.21
  156.7 13.8 %collective-permute-start.13 = (f32[4,128,128]{2,1,0:T(8,128)}, f32[4,128,128]{2,1,0:T(8,128)}, u32[]{:S(2)}, u32[]{:S(2)}) collective-permute-start(f32[4,128,128]{2,1,0:T(8,128)} %bitcast.44), channel_id=1, source_target_pairs={{0,1},{1,2},{2,3},{4,5},{5,6},{6,7},{8,9},{9,10},{10,11},{12,13},{... | collective-permute-start | bytes 786440 | tf_op jit(solution)/shard_map/ppermute | solution.py:16
  159.3 6.4 %copy-start.25 = (f32[1,1,512]{2,1,0:T(1,128)S(1)}, f32[1,1,512]{2,1,0:T(1,128)}, u32[]{:S(2)}) copy-start(f32[1,1,512]{2,1,0:T(1,128)} %get-tuple-element.74) | copy-start | bytes 6148
  159.3 11.2 %collective-permute-start.12 = (f32[4,128,128]{2,1,0:T(8,128)}, f32[4,128,128]{2,1,0:T(8,128)}, u32[]{:S(2)}, u32[]{:S(2)}) collective-permute-start(f32[4,128,128]{2,1,0:T(8,128)} %bitcast.43), channel_id=1, source_target_pairs={{1,0},{2,1},{3,2},{5,4},{6,5},{7,6},{9,8},{10,9},{11,10},{13,12},{... | collective-permute-start | bytes 786440 | tf_op jit(solution)/shard_map/ppermute | solution.py:17
  170.5 1.9 copy-start.6
  172.4 8.5 %copy-start = (f32[131072]{0:T(1024)S(1)}, f32[131072]{0:T(1024)}, u32[]{:S(2)}) copy-start(f32[131072]{0:T(1024)} %scatter_fusion.2) | copy-start | bytes 1572868
  172.4 8.5 %copy-start.9 = (f32[131072]{0:T(1024)S(1)}, f32[131072]{0:T(1024)}, u32[]{:S(2)}) copy-start(f32[131072]{0:T(1024)} %copy-done.7) | copy-start | bytes 1572868
  180.9 10.1 %copy-start.1 = (f32[131072]{0:T(1024)S(1)}, f32[131072]{0:T(1024)}, u32[]{:S(2)}) copy-start(f32[131072]{0:T(1024)} %scatter_fusion.2) | copy-start | bytes 1572868
  180.9 10.2 %copy-start.10 = (f32[131072]{0:T(1024)S(1)}, f32[131072]{0:T(1024)}, u32[]{:S(2)}) copy-start(f32[131072]{0:T(1024)} %copy-done.7) | copy-start | bytes 1572868
  180.9 10.2 %copy-start.12 = (f32[131072]{0:T(1024)S(1)}, f32[131072]{0:T(1024)}, u32[]{:S(2)}) copy-start(f32[131072]{0:T(1024)} %copy-done.11) | copy-start | bytes 1572868
  184.2 5.5 %copy-start.19 = (f32[8,128,128]{2,1,0:T(8,128)}, f32[8,128,128]{2,1,0:T(8,128)S(1)}, u32[]{:S(2)}) copy-start(f32[8,128,128]{2,1,0:T(8,128)S(1)} %get-tuple-element.57) | copy-start | bytes 1572868
  185.2 34.1 %collective-permute-start.15 = (f32[4,128,128]{2,1,0:T(8,128)}, f32[4,128,128]{2,1,0:T(8,128)S(1)}, u32[]{:S(2)}, u32[]{:S(2)}) collective-permute-start(f32[4,128,128]{2,1,0:T(8,128)} %get-tuple-element.56), channel_id=1, source_target_pairs={{0,1},{1,2},{2,3},{4,5},{5,6},{6,7},{8,9},{9,10},{10,11},{12,13},{... | collective-permute-start | bytes 786440 | tf_op jit(solution)/shard_map/ppermute | solution.py:16
  189.7 29.5 %collective-permute-start.14 = (f32[4,128,128]{2,1,0:T(8,128)}, f32[4,128,128]{2,1,0:T(8,128)}, u32[]{:S(2)}, u32[]{:S(2)}) collective-permute-start(f32[4,128,128]{2,1,0:T(8,128)} %get-tuple-element.55), channel_id=1, source_target_pairs={{1,0},{2,1},{3,2},{5,4},{6,5},{7,6},{9,8},{10,9},{11,10},{13,12},{... | collective-permute-start | bytes 786440 | tf_op jit(solution)/shard_map/ppermute | solution.py:17
  195.9 25.1 %copy-start.2 = (f32[131072]{0:T(1024)S(1)}, f32[131072]{0:T(1024)}, u32[]{:S(2)}) copy-start(f32[131072]{0:T(1024)} %scatter_fusion.2) | copy-start | bytes 1572868
  221.0 4.9 %copy-start.24 = (f32[1,1,512]{2,1,0:T(1,128)S(1)}, f32[1,1,512]{2,1,0:T(1,128)}, u32[]{:S(2)}) copy-start(f32[1,1,512]{2,1,0:T(1,128)} %get-tuple-element.71) | copy-start | bytes 6148
Sparse Core Ops, SparseCore 0:
  184.4 34.3 reduce-scatter.1
where the time goes:
time: 241 us; the launch traced here: 240 us
  other arithmetic  104 us (43%)
  starting transfers between devices  48 us (20%)
  local copies, waits for them, and re-layouts  28.5 us (12%)
  blocking collectives  22.6 us (9%)
  waiting for transfers between devices  19.7 us (8%)
  between operations  16.6 us (7%)
    add x4, other arithmetic, advance(): 2.0 * current_ext[4:-4] - before + courant * laplace(current_ext)  33 us
    ppermute x8, starting transfers between devices, padded_2(): before = lax.ppermute(last, axis, up)  30.6 us
    scatter-add x8, other arithmetic, inject(): flattened = field.reshape(-1).at[target].add(values, mode='drop')  27.3 us
    unnamed x1, blocking collectives  22.6 us
    add x4, other arithmetic, retreat(): earlier = 2.0 * current - following + laplace(weighted_ext)  16.6 us
    ppermute x8, waiting for transfers between devices, padded_2(): after = lax.ppermute(initial, axis, down)  16.3 us
    concatenate x8, other arithmetic, padded_2(): array = jnp.concatenate([before, array, after], axis=dim)  14.5 us
    ppermute x8, starting transfers between devices, padded_2(): after = lax.ppermute(initial, axis, down)  10.8 us
  transfers between devices with their start and end apart: 18, of which 5 were waited for; matrix products, arithmetic and copies ran while one was open for 31% of the time, Pallas kernels for 0%

commit v1 on v0

v1 whole, which is shorter than its diff:
```python
import functools

import jax
import jax.numpy as jnp
import ml_dtypes
import numpy as np
from jax import lax
from jax.experimental import pallas as pl
from jax.experimental.pallas import tpu as pltpu
from jax.sharding import PartitionSpec as P

STENCIL = (-205.0 / 72.0, 8.0 / 5.0, -1.0 / 5.0, 8.0 / 315.0, -1.0 / 560.0)
BF = jnp.bfloat16
F32 = jnp.float32
MESH = pl.DeviceIdType.MESH


def halves(value):
    high = float(np.asarray(value, ml_dtypes.bfloat16))
    low = float(np.asarray(value - high, ml_dtypes.bfloat16))
    return high, low


def split(value):
    high = value.astype(BF)
    return high, (value - high.astype(F32)).astype(BF)


def band(size, part, centre):
    gap = jnp.abs(
        lax.broadcasted_iota(jnp.int32, (size, size), 0)
        - lax.broadcasted_iota(jnp.int32, (size, size), 1)
    )
    out = jnp.zeros((size, size), F32)
    if centre:
        out = jnp.where(gap == 0, halves(3.0 * STENCIL[0])[part], out)
    for k in range(1, 5):
        out = jnp.where(gap == k, halves(STENCIL[k])[part], out)
    return out.astype(BF)


def dot(a, b):
    return jnp.dot(a, b, preferred_element_type=F32)


def kernel(
    n, shots, cap,
    pack, where, source, wave,
    courant, blocks, adj, receivers, residual, check_rows,
    grad_out, carry, check_out,
    fp, fw, halo, p0, q3, q2, aq, dp, inj, grad, check, rs, rs_check,
    out1, out0, in1, in0, wz, wy, bt,
    halo_send, halo_recv, a2a_send, a2a_recv, rs_send, rs_recv,
):
    steps = residual.shape[0]
    length, height, breadth = courant.shape
    nrec = residual.shape[1]
    pos = lax.axis_index("space")
    shot = lax.axis_index("shot")
    rows = height // shots
    check_each = check_rows.shape[0] // shots

    barrier = pltpu.get_barrier_semaphore()
    for off in range(1, n):
        pl.semaphore_signal(
            barrier, inc=1, device_id={"space": lax.rem(pos + off, n)}, device_id_type=MESH
        )
    for off in range(1, shots):
        pl.semaphore_signal(
            barrier, inc=1, device_id={"shot": lax.rem(shot + off, shots)}, device_id_type=MESH
        )

    def halo_copy(chain, level, side):
        src = (fp, fw)[chain]
        first = 4 if side == 0 else 8
        peer = lax.rem(pos + (n - 1 if side == 0 else 1), n)
        return pltpu.make_async_remote_copy(
            src_ref=src.at[level, pl.ds(first, 4)],
            dst_ref=halo.at[chain, level, 1 - side],
            send_sem=halo_send.at[chain, level, side],
            recv_sem=halo_recv.at[chain, level, 1 - side],
            device_id={"space": peer},
            device_id_type=MESH,
        )

    def has(side):
        return pos > 0 if side == 0 else pos < n - 1

    def send_halo(chain, level, side):
        @pl.when(has(side))
        def _():
            halo_copy(chain, level, side).start()

    def wait_halo(chain, level, side):
        @pl.when(has(side))
        def _():
            halo_copy(chain, level, 1 - side).wait_recv()

    def wait_sent(chain, level, side):
        @pl.when(has(side))
        def _():
            halo_copy(chain, level, side).wait_send()

    def a2a_copy(level, off):
        src, dst = ((out0, in0), (out1, in1))[level]
        return pltpu.make_async_remote_copy(
            src_ref=src.at[pl.ds(off * cap, cap)],
            dst_ref=dst.at[pl.ds(off * cap, cap)],
            send_sem=a2a_send.at[level, off],
            recv_sem=a2a_recv.at[level, off],
            device_id={"space": lax.rem(pos + off, n)},
            device_id_type=MESH,
        )

    def first_weight(x, c):
        fw[0, x + 4] = courant[x] * adj[1, x]
        return c

    lax.fori_loop(0, length, first_weight, 0)

    def do_pack(level):
        src, dst = ((out0, in0), (out1, in1))[level]

        def own(i, c):
            for u in range(8):
                dst[i * 8 + u] = blocks[level, pack[i * 8 + u]]
            return c

        def other(i, c):
            for u in range(8):
                src[i * 8 + u] = blocks[level, pack[i * 8 + u]]
            return c

        lax.fori_loop(0, cap // 8, own, 0)
        lax.fori_loop(cap // 8, n * cap // 8, other, 0)

    do_pack(1)
    pl.semaphore_wait(barrier, n - 1 + shots - 1)
    for side in range(2):
        send_halo(1, 0, side)
    for off in range(1, n):
        a2a_copy(1, off).start()
    do_pack(0)
    for off in range(1, n):
        a2a_copy(0, off).start()

    def zero(i, c):
        blank = jnp.zeros((height, breadth), F32)
        for level in range(steps):
            for f in (fp, fw):
                f[level, i] = blank
                f[level, i + 4 + length] = blank
        return c

    lax.fori_loop(0, 4, zero, 0)
    for side in range(2):
        @pl.when(jnp.logical_not(has(side)))
        def _():
            def blank(i, c):
                for level in range(steps):
                    for chain in range(2):
                        halo[chain, level, side, i] = jnp.zeros((height, breadth), F32)
                return c

            lax.fori_loop(0, 4, blank, 0)

    for part in range(2):
        z = band(breadth, part, True)
        y = band(height, part, False)
        for k in range(2):
            wz[k * breadth:(k + 1) * breadth, part * breadth:(part + 1) * breadth] = z
            wy[part * height:(part + 1) * height, k * height:(k + 1) * height] = y

    local = receivers[...] - pos * (length * height * breadth)
    rec_row = local // breadth
    rec_col = local - rec_row * breadth
    column = lax.broadcasted_iota(jnp.int32, (breadth, nrec), 0) == rec_col
    for s in range(steps):
        value = residual[s:s + 1, :]
        high = value.astype(BF).astype(F32)
        for k, v in enumerate((high, value - high)):
            bt[s * breadth:(s + 1) * breadth, k * nrec:(k + 1) * nrec] = jnp.where(
                column, v, 0.0
            ).astype(BF)

    def fill_inj(x, c):
        line = lax.broadcasted_iota(jnp.int32, (height, nrec), 0) + x * height
        hot = jnp.where(line == rec_row, 1.0, 0.0).astype(BF)
        got = lax.dot_general(
            jnp.concatenate([hot, hot], axis=1), bt[...], (((1,), (1,)), ((), ())),
            preferred_element_type=F32,
        )
        for s in range(steps):
            inj[s, x] = got[:, s * breadth:(s + 1) * breadth]
        return c

    lax.fori_loop(0, length, fill_inj, 0)

    def spatial(f, level, x):
        plane = f[level, x + 4]
        high, low = split(plane)
        oz = dot(jnp.concatenate([high, low], axis=1), wz[...])
        oy = dot(wy[...], jnp.concatenate([high, low], axis=0))
        acc = (oz[:, :breadth] + oz[:, breadth:]) + (oy[:height] + oy[height:])
        for k in range(1, 5):
            acc = acc + STENCIL[k] * (f[level, x + 4 + k] + f[level, x + 4 - k])
        return acc

    qs = [adj.at[0], adj.at[1]]
    for m in range(steps - 2):
        qs.append((q3, q2)[m] if m < 2 else None)
    qs += [carry.at[0], carry.at[1]]

    def prep_q(level):
        def one(x, c):
            aq[x] = (
                (2.0 * qs[level + 1][x] - qs[level][x])
                + inj[steps - 1 - level, x]
                + spatial(fw, level, x)
            )
            return c

        lax.fori_loop(0, length, one, 0, unroll=2)

    src_local = source[0] - pos * (length * height * breadth)

    def prep_p(level):
        flat = (
            lax.broadcasted_iota(jnp.int32, (height, breadth), 0) * breadth
            + lax.broadcasted_iota(jnp.int32, (height, breadth), 1)
        )
        amount = wave[level]

        def one(x, c):
            hit = flat == src_local - x * (height * breadth)
            dp[level, x] = courant[x] * spatial(fp, level, x) + jnp.where(hit, amount, 0.0)
            return c

        lax.fori_loop(0, length, one, 0, unroll=2)

    def beyond(chain, level, side, i):
        total = None
        for k in range(i + 1, 5):
            at = 4 + i - k if side == 0 else k - i - 1
            term = STENCIL[k] * halo[chain, level, side, at]
            total = term if total is None else total + term
        return total

    def finish_q(level):
        for side in range(2):
            wait_halo(1, level, side)
            for i in range(4):
                x = i if side == 0 else length - 1 - i
                value = aq[x] + beyond(1, level, side, i)
                qs[level + 2][x] = value
                if level + 1 < steps:
                    fw[level + 1, x + 4] = courant[x] * value
            if level + 1 < steps:
                send_halo(1, level + 1, side)

    def finish_p(level):
        for side in range(2):
            wait_halo(0, level, side)
            for i in range(4):
                x = i if side == 0 else length - 1 - i
                change = dp[level, x] + courant[x] * beyond(0, level, side, i)
                if level + 1 < steps:
                    dp[level, x] = change
                    older = p0[x] if level == 0 else fp[level - 1, x + 4]
                    fp[level + 1, x + 4] = (2.0 * fp[level, x + 4] - older) + change
                else:
                    grad[x] = grad[x] + qs[1][x] * change
            if level + 1 < steps:
                send_halo(0, level + 1, side)

    def unpack(level, store):
        got = (in0, in1)[level]
        for off in range(1, n):
            a2a_copy(level, off).wait_recv()
        per_plane = height // 8

        def one(x, c):
            for r in range(per_plane):
                store(x, r, got[where[x * per_plane + r]])
            return c

        lax.fori_loop(0, length, one, 0)

    def store1(x, r, value):
        fp[0, x + 4, r * 8:(r + 1) * 8, :] = value

    def store0(x, r, value):
        p0[x, r * 8:(r + 1) * 8, :] = value

    prep_q(0)
    finish_q(0)
    unpack(1, store1)
    for side in range(2):
        send_halo(0, 0, side)
    prep_q(1)
    prep_p(0)
    finish_q(1)
    prep_q(2)
    unpack(0, store0)
    for level in range(steps - 1):
        finish_p(level)
        prep_p(level + 1)
        if level + 2 < steps - 1:
            finish_q(level + 2)
            prep_q(level + 3)

    def early(x, c):
        total = qs[steps][x] * dp[0, x]
        for m in range(1, steps - 1):
            total = total + qs[steps - m][x] * dp[m, x]
        grad[x] = total
        return c

    lax.fori_loop(0, length, early, 0)

    line = lax.broadcasted_iota(jnp.int32, (check_rows.shape[0], length * height), 1)
    chosen = check_rows[...]
    counts = jnp.zeros(line.shape, F32)
    for k in range(chosen.shape[1]):
        counts = counts + jnp.where(line == chosen[:, k:k + 1], 1.0, 0.0)
    counts = counts.astype(BF)

    finish_p(steps - 1)

    def rs_copy(off):
        peer = lax.rem(shot + off, shots)
        return pltpu.make_async_remote_copy(
            src_ref=grad.at[:, pl.ds(pl.multiple_of(peer * rows, rows), rows), :],
            dst_ref=rs.at[off],
            send_sem=rs_send.at[0, off],
            recv_sem=rs_recv.at[0, off],
            device_id={"shot": peer},
            device_id_type=MESH,
        )

    def rs_check_copy(off):
        peer = lax.rem(shot + off, shots)
        return pltpu.make_async_remote_copy(
            src_ref=check.at[pl.ds(pl.multiple_of(peer * check_each, check_each), check_each), :],
            dst_ref=rs_check.at[off],
            send_sem=rs_send.at[1, off],
            recv_sem=rs_recv.at[1, off],
            device_id={"shot": peer},
            device_id_type=MESH,
        )

    for off in range(1, shots):
        rs_copy(off).start()
    high, low = split(grad[...].reshape(length * height, breadth))
    both = dot(counts, jnp.concatenate([high, low], axis=1))
    check[...] = both[:, :breadth] + both[:, breadth:]
    for off in range(1, shots):
        rs_check_copy(off).start()

    finish_q(steps - 1)

    total = grad[:, pl.ds(pl.multiple_of(shot * rows, rows), rows), :]
    for off in range(1, shots):
        rs_copy(off).wait_recv()
        total = total + rs[off]
    grad_out[...] = total
    total = check[pl.ds(pl.multiple_of(shot * check_each, check_each), check_each), :]
    for off in range(1, shots):
        rs_check_copy(off).wait_recv()
        total = total + rs_check[off]
    check_out[...] = total

    for chain in range(2):
        for level in range(steps):
            for side in range(2):
                wait_sent(chain, level, side)
    for level in range(2):
        for off in range(1, n):
            a2a_copy(level, off).wait_send()
    for off in range(1, shots):
        rs_copy(off).wait_send()
        rs_check_copy(off).wait_send()


def tables(targets, n, cap, per_device, pos):
    grid = targets.reshape(n, per_device)
    peers = grid // per_device
    order = jnp.arange(per_device, dtype=jnp.int32)
    same = (peers[:, :, None] == peers[:, None, :]) & (order[None, None, :] < order[None, :, None])
    rank = jnp.sum(same.astype(jnp.int32), axis=2)
    sender = jnp.arange(n, dtype=jnp.int32)[:, None]
    slot = ((peers - sender + n) % n) * cap + rank
    own = lax.dynamic_index_in_dim(slot, pos, 0, keepdims=False)
    slots = jnp.arange(n * cap, dtype=jnp.int32)
    pack = jnp.sum(jnp.where(own[None, :] == slots[:, None], order[None, :], 0), axis=1)
    mine = pos * per_device + order
    where = jnp.sum(
        jnp.where(targets[None, :] == mine[:, None], slot.reshape(1, -1), 0), axis=1
    )
    return pack, where


def body(
    courant, checkpoint, block_target, adjoint_state, wavelet, source_cell,
    receiver_cell, residual, check_rows,
):
    n = lax.axis_size("space")
    shots = lax.axis_size("shot")
    length, height, breadth = courant.shape
    per_device = checkpoint.shape[2]
    cap = per_device // 4
    steps = wavelet.shape[1]
    chk = check_rows.shape[1]
    nrec = residual.shape[2]
    pack, where = tables(block_target[0], n, cap, per_device, lax.axis_index("space"))

    smem = pl.BlockSpec(memory_space=pltpu.SMEM)
    vmem = pl.BlockSpec(memory_space=pltpu.VMEM)
    slab = (length, height, breadth)
    buf = lambda *shape: pltpu.VMEM(shape, F32)
    blk = checkpoint.shape[3:]
    dma = pltpu.SemaphoreType.DMA
    grad, carry, check = pl.pallas_call(
        functools.partial(kernel, n, shots, cap),
        out_shape=(
            jax.ShapeDtypeStruct((length, height // shots, breadth), F32),
            jax.ShapeDtypeStruct((2,) + slab, F32),
            jax.ShapeDtypeStruct((chk // shots, breadth), F32),
        ),
        in_specs=[smem] * 4 + [vmem] * 6,
        out_specs=(vmem,) * 3,
        scratch_shapes=[
            buf(steps, length + 8, height, breadth),
            buf(steps, length + 8, height, breadth),
            buf(2, steps, 2, 4, height, breadth),
            buf(*slab), buf(*slab), buf(*slab), buf(*slab),
            buf(steps, *slab), buf(steps, *slab), buf(*slab),
            buf(chk, breadth),
            buf(shots, length, height // shots, breadth),
            buf(shots, chk // shots, breadth),
            buf(n * cap, *blk), buf(n * cap, *blk), buf(n * cap, *blk), buf(n * cap, *blk),
            pltpu.VMEM((2 * breadth, 2 * breadth), BF),
            pltpu.VMEM((2 * height, 2 * height), BF),
            pltpu.VMEM((steps * breadth, 2 * nrec), BF),
            dma((2, steps, 2)), dma((2, steps, 2)),
            dma((2, n)), dma((2, n)), dma((2, shots)), dma((2, shots)),
        ],
        compiler_params=pltpu.CompilerParams(
            collective_id=0, has_side_effects=True, vmem_limit_bytes=56 * 1024 * 1024
        ),
    )(
        pack, where, source_cell, wavelet[0],
        courant, checkpoint[0], adjoint_state[0], receiver_cell, residual[0], check_rows[0],
    )
    return grad, carry[None], check[None]


def solution(mesh):
    in_specs = (
        P("space", None, None),
        P("shot", None, "space", None, None),
        P("shot", None),
        P("shot", None, "space", None, None),
        P("shot", None),
        P("shot"),
        P("shot", None),
        P("shot", None, None),
        P("space", None, None),
    )
    out_specs = (
        P("space", "shot", None),
        P("shot", None, "space", None, None),
        P("space", "shot", None),
    )
    return jax.shard_map(body, mesh=mesh, in_specs=in_specs, out_specs=out_specs, check_vma=False)
```

time: 241 us -> 92.9 us (0.39)
  the two profiles are of different devices: /device:TPU:0 before, /device:TPU:17 now
where the time goes in v1:
time: 92.9 us; the launch traced here: 92.7 us
  Pallas kernels  83.9 us (90%)
  local copies, waits for them, and re-layouts  5.76 us (6%)
  other arithmetic  1.64 us (2%)
  between operations  1.34 us (1%)
    pallas_call x1, Pallas kernels, body(): pl.pallas_call(functools.partial(kernel, n, shots, cap), out_shape=(jax.S...  83.9 us
    unnamed x10, local copies, waits for them, and re-layouts  5.75 us

profile of v1, /device:TPU:17, one launch (start us, length us, event | category | flops | bytes accessed | tf_op | source)
XLA Modules:
  0.0 92.7 jit_solution(8269211729767131055)
XLA Ops:
  1.3 0.0 copy-start
  1.3 0.7 copy-done
  2.0 0.2 convert_reduce_fusion
  2.3 0.0 copy-start.1
  2.3 0.7 select_reduce_fusion.where
  3.0 0.6 select_reduce_fusion.1.pack
  3.7 0.0 copy-done.1
  3.7 0.7 copy.13
  4.4 83.9 %shard_map.112 = (f32[8,16,128]{2,1,0:T(8,128)}, f32[2,8,128,128]{3,2,1,0:T(8,128)}, f32[8,128]{1,0:T(8,128)}) custom-call(s32[128]{0:T(128)} %select_reduce_fusion.1.pack, s32[128]{0:T(128)} %select_reduce_fusion.where, s32[1]{0:T(128)S(6)} %copy.17.source, f32[4]{0:T(128)} %bitcast.26, f32[8,128,128]{2,1,0:T(8,128)} %courant.1, ...), custom_call_target="tpu_custom_call" | custom-call | tf_op jit(solution)/shard_map/pallas_call | solution.py:423
  88.3 1.5 %copy.18 = f32[8,16,128]{2,1,0:T(8,128)} copy(f32[8,16,128]{2,1,0:T(8,128)} %get-tuple-element.12) | data formatting | bytes 131072
  89.8 0.0 copy-start.2
  89.8 2.3 %copy.19 = f32[1,2,8,128,128]{4,3,2,1,0:T(8,128)} copy(f32[1,2,8,128,128]{4,3,2,1,0:T(8,128)} %bitcast.16) | data formatting | bytes 2097152
  92.1 0.0 copy-done.2
  92.1 0.6 copy.20
  (7 shorter events, 0.1 us)
Async XLA Ops:
  1.3 0.7 copy-start
  2.3 1.4 %copy-start.1 = (s32[1,64,16]{1,2,0:T(8,128)S(1)}, s32[1,64,16]{1,2,0:T(8,128)}, u32[]{:S(2)}) copy-start(s32[1,64,16]{1,2,0:T(8,128)} %param.17) | copy-start | bytes 12292
  89.8 2.3 %copy-start.2 = (f32[8,128]{1,0:T(8,128)S(1)}, f32[8,128]{1,0:T(8,128)}, u32[]{:S(2)}) copy-start(f32[8,128]{1,0:T(8,128)} %get-tuple-element.8) | copy-start | bytes 12292

commit v2 on v1

--- a/solution.py
+++ b/solution.py
@@ -136,10 +136,10 @@
 
     do_pack(1)
     pl.semaphore_wait(barrier, n - 1 + shots - 1)
+    for off in range(1, n):
+        a2a_copy(1, off).start()
     for side in range(2):
         send_halo(1, 0, side)
-    for off in range(1, n):
-        a2a_copy(1, off).start()
     do_pack(0)
     for off in range(1, n):
         a2a_copy(0, off).start()
@@ -255,7 +255,7 @@
                 qs[level + 2][x] = value
                 if level + 1 < steps:
                     fw[level + 1, x + 4] = courant[x] * value
-            if level + 1 < steps:
+            if level + 2 < steps:
                 send_halo(1, level + 1, side)
 
     def finish_p(level):
@@ -293,21 +293,19 @@
         p0[x, r * 8:(r + 1) * 8, :] = value
 
     prep_q(0)
-    finish_q(0)
     unpack(1, store1)
     for side in range(2):
         send_halo(0, 0, side)
+    prep_p(0)
+    finish_q(0)
     prep_q(1)
-    prep_p(0)
-    finish_q(1)
-    prep_q(2)
     unpack(0, store0)
     for level in range(steps - 1):
         finish_p(level)
         prep_p(level + 1)
-        if level + 2 < steps - 1:
-            finish_q(level + 2)
-            prep_q(level + 3)
+        if level + 1 < steps - 1:
+            finish_q(level + 1)
+            prep_q(level + 2)
 
     def early(x, c):
         total = qs[steps][x] * dp[0, x]
@@ -351,6 +349,8 @@
 
     for off in range(1, shots):
         rs_copy(off).start()
+    for side in range(2):
+        send_halo(1, steps - 1, side)
     high, low = split(grad[...].reshape(length * height, breadth))
     both = dot(counts, jnp.concatenate([high, low], axis=1))
     check[...] = both[:, :breadth] + both[:, breadth:]

time: 92.9 us -> 88.9 us (0.957)
  the two profiles are of different devices: /device:TPU:17 before, /device:TPU:0 now
where the time goes in v2:
time: 88.9 us; the launch traced here: 88.7 us
  Pallas kernels  79.9 us (90%)
  local copies, waits for them, and re-layouts  5.76 us (6%)
  other arithmetic  1.64 us (2%)
  between operations  1.34 us (2%)
    pallas_call x1, Pallas kernels, body(): pl.pallas_call(functools.partial(kernel, n, shots, cap), out_shape=(jax.S...  79.9 us
    unnamed x10, local copies, waits for them, and re-layouts  5.75 us

profile of v2, /device:TPU:0, one launch (start us, length us, event | category | flops | bytes accessed | tf_op | source)
XLA Modules:
  0.0 88.7 jit_solution(4772958300991535205)
XLA Ops:
  1.3 0.0 copy-start
  1.3 0.7 copy-done
  2.0 0.2 convert_reduce_fusion
  2.3 0.0 copy-start.1
  2.3 0.7 select_reduce_fusion.where
  3.0 0.6 select_reduce_fusion.1.pack
  3.7 0.0 copy-done.1
  3.7 0.7 copy.13
  4.4 79.9 %shard_map.112 = (f32[8,16,128]{2,1,0:T(8,128)}, f32[2,8,128,128]{3,2,1,0:T(8,128)}, f32[8,128]{1,0:T(8,128)}) custom-call(s32[128]{0:T(128)} %select_reduce_fusion.1.pack, s32[128]{0:T(128)} %select_reduce_fusion.where, s32[1]{0:T(128)S(6)} %copy.17.source, f32[4]{0:T(128)} %bitcast.26, f32[8,128,128]{2,1,0:T(8,128)} %courant.1, ...), custom_call_target="tpu_custom_call" | custom-call | tf_op jit(solution)/shard_map/pallas_call | solution.py:423
  84.3 1.5 %copy.18 = f32[8,16,128]{2,1,0:T(8,128)} copy(f32[8,16,128]{2,1,0:T(8,128)} %get-tuple-element.12) | data formatting | bytes 131072
  85.8 0.0 copy-start.2
  85.8 2.3 %copy.19 = f32[1,2,8,128,128]{4,3,2,1,0:T(8,128)} copy(f32[1,2,8,128,128]{4,3,2,1,0:T(8,128)} %bitcast.16) | data formatting | bytes 2097152
  88.1 0.0 copy-done.2
  88.1 0.6 copy.20
  (7 shorter events, 0.1 us)
Async XLA Ops:
  1.3 0.7 copy-start
  2.3 1.4 %copy-start.1 = (s32[1,64,16]{1,2,0:T(8,128)S(1)}, s32[1,64,16]{1,2,0:T(8,128)}, u32[]{:S(2)}) copy-start(s32[1,64,16]{1,2,0:T(8,128)} %param.17) | copy-start | bytes 12292
  85.8 2.3 %copy-start.2 = (f32[8,128]{1,0:T(8,128)S(1)}, f32[8,128]{1,0:T(8,128)}, u32[]{:S(2)}) copy-start(f32[8,128]{1,0:T(8,128)} %get-tuple-element.8) | copy-start | bytes 12292
